TPU v7x, 128 devices: a whole 4x4x4 slice. The times are simulated.
128 devices in a mesh: row: 8 (over y, core), col: 16 (over z, x).
Axes of the slice: x: 4, y: 4, z: 4, core: 2. Of those that a mesh axis runs over, the one named last changes fastest.
Arguments:
- weights: bfloat16 [8192, 8192], P('row', 'col')
- panel: bfloat16 [8192, 8192], P('row', 'col'), may hold values from 0.0099487305 to 1
- pattern: int32 [32, 32], P('row', 'col'), may hold values from 0 to 1, as said below
Outputs:
- flow: float32 [8192, 8192], P('row', 'col')
Inputs may be any that keep to these rules, and one draw needn't show every extreme that they name: `pattern`: 0 or 1; each device's block of 4 x 2 tiles holds 1 to 4 ones, and some block holds exactly 4.
All inputs are finite; a program needn't handle non-finite values.
Results may differ from a plain program's by a relative error of at most 0.0003.
Values may be sent and summed in bfloat16 or wider, within the bound.
A program may use at most 128 MiB of HBM per device.

v0:
```python
import jax
import jax.numpy as jnp
from jax import lax
from jax.sharding import PartitionSpec as P

TILE = 256


def local(weights, panel, pattern):
    full_panel = lax.all_gather(panel, "row", axis=0, tiled=True)
    grown = jnp.repeat(jnp.repeat(pattern, TILE, axis=0), TILE, axis=1)
    masked = weights * grown.astype(jnp.bfloat16)
    expanded = jnp.dot(
        lax.all_gather(masked, "col", axis=1, tiled=True),
        full_panel,
        preferred_element_type=jnp.float32,
    )
    inflated = expanded * expanded
    totals = lax.psum(jnp.sum(inflated, axis=0), "row")
    nodes = jnp.float32(full_panel.shape[0])
    return nodes * inflated / totals[None, :]


def solution(mesh):
    in_specs = (P("row", "col"), P("row", "col"), P("row", "col"))
    out_specs = P("row", "col")
    return jax.shard_map(local, mesh=mesh, in_specs=in_specs, out_specs=out_specs, check_vma=False)
```

profile of v0, /device:TPU:1, one launch (start us, length us, event | category | flops | bytes accessed | tf_op | source)
XLA Modules:
  0.0 220.8 jit_solution(1552896682880659229)
XLA Ops:
  6.5 0.0 all-gather.5.cloned.1.call-start
  6.5 0.7 all-gather.5.cloned.1.call-update
  7.3 0.0 copy-start
  7.3 0.0 all-gather.3.cloned.1.call-start
  7.3 0.8 convert_element_type.11
  8.1 0.1 copy.4
  8.2 1.2 broadcast_in_dim.8
  9.5 0.2 copy.5
  9.7 0.0 copy-done
  9.7 1.3 mul.12
  11.0 0.0 all-gather.3.cloned.1.call-update
  11.0 51.4 %all-gather.5.cloned.1.call-done = bf16[8192,512]{1,0:T(8,128)(2,1)} async-done(((bf16[1024,512]{1,0:T(8,128)(2,1)}), bf16[8192,512]{1,0:T(8,128)(2,1)}) %all-gather.5.cloned.1.call-update) | async-done | bytes 8388624 | tf_op jit(solution)/shard_map/all_gather | solution.py:10
  62.5 122.2 %all-gather.3.cloned.1.call-done = bf16[1024,8192]{1,0:T(8,128)(2,1)} async-done(((bf16[1024,512]{1,0:T(8,128)(2,1)}), bf16[1024,8192]{1,0:T(8,128)(2,1)}) %all-gather.3.cloned.1.call-update) | async-done | bytes 16777232 | tf_op jit(solution)/shard_map/all_gather | solution.py:14
  184.7 14.4 %multiply_reduce_fusion = (f32[512]{0:T(512)S(1)}, f32[1024,512]{1,0:T(8,128)S(1)}) fusion(bf16[1024,8192]{1,0:T(8,128)(2,1)} %all-gather.3.cloned.1.call-done, bf16[8192,512]{1,0:T(8,128)(2,1)} %all-gather.5.cloned.1.call-done), kind=kOutput, calls=%fused_computation.1 | convolution fusion | flops 8590983168 | bytes 27265024 | tf_op jit(solution)/shard_map/dot_general | solution.py:13
  199.0 13.3 %psum.7 = f32[512]{0:T(512)S(1)} all-reduce(f32[512]{0:T(512)S(1)} %get-tuple-element.5), channel_id=1, replica_groups=mesh['row'=8,'col'=16] {'row'}, use_global_device_ids=true, to_apply=%region_1.0 | all-reduce | flops 512 | bytes 4096 | tf_op jit(solution)/shard_map/psum | solution.py:19
  212.3 1.6 multiply_divide_fusion
  (1 shorter events, 0.0 us)
Async XLA Ops:
  6.5 55.9 %all-gather.5.cloned.1.call-start = ((), (), s32[]{:S(2)}) async-start(), calls=%async_computation.1 | async-start | bytes 9437184 | tf_op jit(solution)/shard_map/all_gather | solution.py:10
  7.3 2.5 %copy-start = (bf16[1024,512]{1,0:T(8,128)(2,1)S(1)}, bf16[1024,512]{1,0:T(8,128)(2,1)}, u32[]{:S(2)}) copy-start(bf16[1024,512]{1,0:T(8,128)(2,1)} %param.3) | copy-start | bytes 3145732
  7.3 177.4 %all-gather.3.cloned.1.call-start = ((), (), s32[]{:S(2)}) async-start(), calls=%async_computation | async-start | bytes 17825792 | tf_op jit(solution)/shard_map/all_gather | solution.py:14
Sparse Core Ops, SparseCore 0:
  9.1 53.3 all-gather.4
  64.6 120.0 all-gather.2
where the time goes:
time: 221 us
  waiting for transfers between devices  174 us (79%)
  matrix products  14.4 us (7%)
  between operations  13.4 us (6%)
  blocking collectives  13.3 us (6%)
  other arithmetic  3.65 us (2%)
    all_gather x1, waiting for transfers between devices, local(): lax.all_gather(masked, 'col', axis=1, tiled=True)  122 us
    all_gather x1, waiting for transfers between devices, local(): full_panel = lax.all_gather(panel, 'row', axis=0, tiled=True)  51.4 us
    dot_general x1, matrix products, local(): jnp.dot(lax.all_gather(masked, 'col', axis=1, tiled=True), full_panel, pr...  14.4 us
    psum x1, blocking collectives, local(): totals = lax.psum(jnp.sum(inflated, axis=0), 'row')  13.3 us
  transfers between devices with their start and end apart: 2, of which 2 were waited for; matrix products, arithmetic and copies ran while one was open for 2% of the time, Pallas kernels for 0%

commit v1 on v0

v1 whole, which is shorter than its diff:
```python
import functools

import jax
import jax.numpy as jnp
from jax import lax
from jax.experimental import pallas as pl
from jax.experimental.pallas import tpu as pltpu
from jax.sharding import PartitionSpec as P

TILE = 256
MESH = pl.DeviceIdType.MESH
SIDE = 4
SLOTS = 4
COMPUTE = True

TREE = (
    ((1, 0), (0, 0)),
    ((-1, 0), (0, 0)),
    ((0, 1), (0, 0)),
    ((0, -1), (0, 0)),
    ((1, 1), (1, 0)),
    ((-1, -1), (-1, 0)),
    ((-1, 1), (0, 1)),
    ((1, -1), (0, -1)),
    ((2, 1), (1, 1)),
    ((-1, 2), (-1, 1)),
    ((2, -1), (1, -1)),
    ((1, 2), (1, 1)),
    ((2, 0), (1, 0)),
    ((0, 2), (0, 1)),
    ((2, 2), (2, 1)),
)
ROUNDS = len(TREE)
LAG = 3
STEPS = 6
UP = (0, 1, 2, 3, 0, 1)
DOWN = (2, 3, 0, 1, 2, 3)


def turn(offset, times):
    dx, dz = offset
    for _ in range(times):
        dx, dz = -dz, dx
    return dx, dz


def handled(step):
    return 2 * step + 1


def compute_plan():
    arrive = {(0, 0): 2}
    for number, (offset, _) in enumerate(TREE):
        for s in range(SLOTS):
            dx, dz = turn(offset, s)
            key = (dx % SIDE, dz % SIDE)
            arrive[key] = max(arrive.get(key, 0), number + 1 + LAG)
    last = ROUNDS + LAG
    orders = {}
    ready = {}
    for delta in range(SIDE):
        for parity in range(2):
            when = {}
            for (dx, dz), t in arrive.items():
                dy = (delta - dz) % SIDE
                quarter = (parity + dx) % 2
                if dy == 0:
                    b = 3
                elif dy == 2:
                    b = handled(6) + 1
                elif dy == 3:
                    b = handled(2 if quarter == 0 else 4) + 1
                else:
                    b = handled(2 if quarter == 1 else 4) + 1
                when[(dx, dz)] = max(t, b)
            order = sorted(when, key=lambda o: (when[o], o))
            orders[delta, parity] = order
            ready[delta, parity] = [when[o] for o in order]
    counts = {}
    done = 0
    for t in range(1, last + 1):
        able = min(sum(1 for w in ready[v] if w <= t) for v in ready) - done
        take = able if t > ROUNDS else min(able, 2)
        counts[t] = take
        done += take
    assert done == SIDE * SIDE
    return orders, counts


ORDERS, COUNTS = compute_plan()


def kernel(
    pattern_ref, weights_ref, panel_ref, out_ref, sums_ref,
    own, graph, panel, meta, total, part, parts,
    local_sem, out_sem, a_send, a_recv, b_send, b_recv, c_send, c_recv,
    m_send, m_recv, t_send, t_recv,
):
    row, col = lax.axis_index("row"), lax.axis_index("col")
    y, core = row // 2, row % 2
    z, x = col // SIDE, col % SIDE

    def wrap(v):
        return (v + 2 * SIDE) % SIDE

    def at(dx, dz):
        return wrap(z + dz) * SIDE + wrap(x + dx)

    def lane(dy):
        return wrap(y + dy) * 2 + core

    other = y * 2 + 1 - core

    load_a = pltpu.make_async_copy(weights_ref, own, local_sem.at[0])
    load_a.start()
    mine = pl.multiple_of(row * 4, 4)
    load_b = pltpu.make_async_copy(panel_ref, panel.at[pl.ds(mine, 4)], local_sem.at[1])
    load_b.start()

    barrier = pltpu.get_barrier_semaphore()
    for i in range(1, 16):
        pl.semaphore_signal(barrier, inc=1, device_id=(row, (col + i) % 16), device_id_type=MESH)
    for i in range(1, 8):
        pl.semaphore_signal(barrier, inc=1, device_id=((row + i) % 8, col), device_id_type=MESH)

    bits = [pattern_ref[i // 2, i % 2] for i in range(8)]
    code = functools.reduce(lambda a, b: a + b, [bits[i] << i for i in range(8)])
    meta[col, 0] = code

    load_a.wait()
    ranks = [jnp.int32(0)]
    for i in range(7):
        ranks.append(ranks[-1] + bits[i])
    for s in range(SLOTS):
        tile = jnp.zeros((TILE, TILE), jnp.bfloat16)
        for i in range(s, 8):
            r, c = i // 2 * TILE, i % 2 * TILE
            tile = jnp.where((bits[i] == 1) & (ranks[i] == s), own[r:r + TILE, c:c + TILE], tile)
        graph[col, s] = tile
    load_b.wait()
    pl.semaphore_wait(barrier, 22)

    def meta_copy(i):
        return pltpu.make_async_remote_copy(
            src_ref=meta.at[col], dst_ref=meta.at[col],
            send_sem=m_send.at[i - 1], recv_sem=m_recv.at[i - 1],
            device_id=(row, (col + i) % 16), device_id_type=MESH)

    def meta_arrival(i):
        source = (col - i + 16) % 16
        return pltpu.make_async_remote_copy(
            src_ref=meta.at[source], dst_ref=meta.at[source],
            send_sem=m_send.at[i - 1], recv_sem=m_recv.at[i - 1],
            device_id=(row, source), device_id_type=MESH)

    def a_copy(number, s):
        offset, parent = TREE[number]
        px, pz = turn(parent, s)
        dx, dz = turn((offset[0] - parent[0], offset[1] - parent[1]), s)
        source = at(-px, -pz)
        return pltpu.make_async_remote_copy(
            src_ref=graph.at[source, s], dst_ref=graph.at[source, s],
            send_sem=a_send.at[number, s], recv_sem=a_recv.at[number, s],
            device_id=(row, at(dx, dz)), device_id_type=MESH)

    def a_arrival(number, s):
        offset, _ = TREE[number]
        dx, dz = turn(offset, s)
        source = at(-dx, -dz)
        return pltpu.make_async_remote_copy(
            src_ref=graph.at[source, s], dst_ref=graph.at[source, s],
            send_sem=a_send.at[number, s], recv_sem=a_recv.at[number, s],
            device_id=(row, col), device_id_type=MESH)

    def b_piece(way, step, received):
        j = (UP if way > 0 else DOWN)[step - 1]
        hops = (1 if received else 0) + (1 if step > 4 else 0)
        return lane(-way * hops) * 4 + j

    def b_copy(way, step):
        piece = b_piece(way, step, False)
        n = 0 if way > 0 else 1
        return pltpu.make_async_remote_copy(
            src_ref=panel.at[piece], dst_ref=panel.at[piece],
            send_sem=b_send.at[step - 1, n], recv_sem=b_recv.at[step - 1, n],
            device_id=(lane(way), col), device_id_type=MESH)

    def b_arrival(way, step):
        piece = b_piece(way, step, True)
        n = 0 if way > 0 else 1
        return pltpu.make_async_remote_copy(
            src_ref=panel.at[piece], dst_ref=panel.at[piece],
            send_sem=b_send.at[step - 1, n], recv_sem=b_recv.at[step - 1, n],
            device_id=(row, col), device_id_type=MESH)

    def c_piece(step, n, theirs):
        if step == 0:
            lane_row, j = lane(0), n
        else:
            way = 1 if n == 0 else -1
            hops = 2 if step > 4 else 1
            lane_row, j = lane(-way * hops), (UP if way > 0 else DOWN)[step - 1]
        if theirs:
            lane_row = (lane_row // 2) * 2 + 1 - core
        return lane_row * 4 + j

    def c_copy(step, n, theirs=False):
        piece = c_piece(step, n, theirs)
        k = n if step == 0 else 2 + 2 * step + n
        return pltpu.make_async_remote_copy(
            src_ref=panel.at[piece], dst_ref=panel.at[piece],
            send_sem=c_send.at[k], recv_sem=c_recv.at[k],
            device_id=(other, col), device_id_type=MESH)

    def c_range(step):
        return range(4 if step == 0 else 2)

    def ordered(place):
        index = jnp.int32(0)
        variant = wrap(z - y) * 2 + x % 2
        for v in range(8):
            dx, dz = ORDERS[v // 2, v % 2][place]
            index = jnp.where(variant == v, at(-dx, -dz), index)
        return index

    def add_source(source, first):
        present = meta[source, 0]
        have = [(present >> i) & 1 for i in range(8)]
        before = [jnp.int32(0)]
        for i in range(7):
            before.append(before[-1] + have[i])
        tiles = [graph.at[source, s] for s in range(SLOTS)]
        piece = pl.multiple_of(source * 2, 2)
        for r in range(4):
            sides = []
            for c in range(2):
                i = 2 * r + c
                tile = jnp.zeros((TILE, TILE), jnp.bfloat16)
                for s in range(min(i + 1, SLOTS)):
                    tile = jnp.where((have[i] == 1) & (before[i] == s), tiles[s][...], tile)
                sides.append(tile)
            product = jnp.dot(sides[0], panel[piece], preferred_element_type=jnp.float32)
            product += jnp.dot(sides[1], panel[piece + 1], preferred_element_type=jnp.float32)
            rows = pl.ds(r * TILE, TILE)
            if first:
                total[rows, :] = product
            else:
                total[rows, :] += product

    done = 0
    for t in range(1, ROUNDS + LAG + 1):
        if t == 1:
            for i in range(1, 16):
                meta_copy(i).start()
        if t > LAG:
            for s in range(SLOTS):
                a_arrival(t - LAG - 1, s).wait_recv()
        if t <= ROUNDS:
            for s in range(SLOTS):
                a_copy(t - 1, s).start()
        if t == 1:
            for step in (1, 2):
                for way in (1, -1):
                    b_copy(way, step).start()
            for n in c_range(0):
                c_copy(0, n).start()
        if t == 2:
            for n in c_range(0):
                c_copy(0, n, True).wait_recv()
            for i in range(1, 16):
                meta_arrival(i).wait_recv()
        for step in range(1, STEPS + 1):
            if t == handled(step):
                for way in (1, -1):
                    b_arrival(way, step).wait_recv()
                for n in c_range(step):
                    c_copy(step, n).start()
                if step + 2 <= STEPS:
                    for way in (1, -1):
                        b_copy(way, step + 2).start()
            if t == handled(step) + 1:
                for n in c_range(step):
                    c_copy(step, n, True).wait_recv()
        for _ in range(COUNTS[t]):
            if COMPUTE:
                add_source(ordered(done), done == 0)
            done += 1

    def t_copy(i):
        return pltpu.make_async_remote_copy(
            src_ref=part, dst_ref=parts.at[row],
            send_sem=t_send.at[i - 1], recv_sem=t_recv.at[i - 1],
            device_id=((row + i) % 8, col), device_id_type=MESH)

    def t_arrival(i):
        source = (row - i + 8) % 8
        return pltpu.make_async_remote_copy(
            src_ref=part, dst_ref=parts.at[source],
            send_sem=t_send.at[i - 1], recv_sem=t_recv.at[i - 1],
            device_id=(row, col), device_id_type=MESH)

    sums = jnp.zeros((8, 512), jnp.float32)
    for r in range(4):
        block = total[r * TILE:(r + 1) * TILE, :]
        block = block * block
        total[r * TILE:(r + 1) * TILE, :] = block
        sums += jnp.sum(block.reshape(TILE // 8, 8, 512), axis=0)
    part[...] = sums
    for i in range(1, 8):
        t_copy(i).start()
    store = pltpu.make_async_copy(total, out_ref, out_sem)
    store.start()
    parts[row] = sums

    for i in range(1, 16):
        meta_copy(i).wait_send()
    for number in range(ROUNDS):
        for s in range(SLOTS):
            a_copy(number, s).wait_send()
    for step in range(1, STEPS + 1):
        for way in (1, -1):
            b_copy(way, step).wait_send()
    for step in range(STEPS + 1):
        for n in c_range(step):
            c_copy(step, n).wait_send()

    for i in range(1, 8):
        t_arrival(i).wait_recv()
    whole = parts[0]
    for i in range(1, 8):
        whole += parts[i]
    sums_ref[...] = jnp.sum(whole, axis=0, keepdims=True)
    for i in range(1, 8):
        t_copy(i).wait_send()
    store.wait()


def local(weights, panel, pattern):
    inflated, totals = pl.pallas_call(
        kernel,
        out_shape=(
            jax.ShapeDtypeStruct((1024, 512), jnp.float32),
            jax.ShapeDtypeStruct((1, 512), jnp.float32),
        ),
        in_specs=[
            pl.BlockSpec(memory_space=pltpu.SMEM),
            pl.BlockSpec(memory_space=pl.ANY),
            pl.BlockSpec(memory_space=pl.ANY),
        ],
        out_specs=(
            pl.BlockSpec(memory_space=pl.ANY),
            pl.BlockSpec(memory_space=pltpu.VMEM),
        ),
        scratch_shapes=[
            pltpu.VMEM((1024, 512), jnp.bfloat16),
            pltpu.VMEM((16, SLOTS, TILE, TILE), jnp.bfloat16),
            pltpu.VMEM((32, TILE, 512), jnp.bfloat16),
            pltpu.SMEM((16, 128), jnp.int32),
            pltpu.VMEM((1024, 512), jnp.float32),
            pltpu.VMEM((8, 512), jnp.float32),
            pltpu.VMEM((8, 8, 512), jnp.float32),
            pltpu.SemaphoreType.DMA((2,)),
            pltpu.SemaphoreType.DMA,
            pltpu.SemaphoreType.DMA((ROUNDS, SLOTS)),
            pltpu.SemaphoreType.DMA((ROUNDS, SLOTS)),
            pltpu.SemaphoreType.DMA((STEPS, 2)),
            pltpu.SemaphoreType.DMA((STEPS, 2)),
            pltpu.SemaphoreType.DMA((4 + 2 * STEPS,)),
            pltpu.SemaphoreType.DMA((4 + 2 * STEPS,)),
            pltpu.SemaphoreType.DMA((15,)),
            pltpu.SemaphoreType.DMA((15,)),
            pltpu.SemaphoreType.DMA((7,)),
            pltpu.SemaphoreType.DMA((7,)),
        ],
        compiler_params=pltpu.CompilerParams(
            collective_id=0, has_side_effects=True, vmem_limit_bytes=40 * 1024 * 1024
        ),
        cost_estimate=pl.CostEstimate(
            flops=2 * 1024 * 8192 * 512, bytes_accessed=4 * 1024 * 1024, transcendentals=0
        ),
    )(pattern, weights, panel.reshape(4, TILE, 512))
    nodes = jnp.float32(8192)
    return nodes * inflated / totals


def solution(mesh):
    spec = P("row", "col")
    return jax.shard_map(local, mesh=mesh, in_specs=(spec, spec, spec), out_specs=spec, check_vma=False)
```

time: 221 us -> 66 us (0.30)
  waiting for transfers between devices: 174 us -> 0 us
  Pallas kernels: 0 us -> 61 us
  matrix products: 14.4 us -> 0 us
  between operations: 13.4 us -> 0.01 us
  blocking collectives: 13.3 us -> 0 us
    all_gather x2 -> x0, waiting for transfers between devices: 174 us -> none  [the longest x1 122 us: local(): lax.all_gather(masked, 'col', axis=1, tiled=True)]
    pallas_call x0 -> x1, Pallas kernels: none -> 61 us  [local(): pl.pallas_call(kernel, out_shape=(jax.ShapeDtypeStruct((1024, 512), jnp.f...]
    dot_general x1 -> x0, matrix products: 14.4 us -> none  [local(): jnp.dot(lax.all_gather(masked, 'col', axis=1, tiled=True), full_panel, pr...]
    psum x1 -> x0, blocking collectives: 13.3 us -> none  [local(): totals = lax.psum(jnp.sum(inflated, axis=0), 'row')]
    unnamed x3 -> x5, local copies, waits for them, and re-layouts: 0.24 us -> 3.21 us
  transfers between devices with their start and end apart: 2 -> 0, of which waited for: 2 -> 0; matrix products, arithmetic and copies ran while one was open for 2% -> 0% of each run, Pallas kernels for 0% -> 0%
where the time goes in v1:
time: 66 us; the launch traced here: 65.8 us
  Pallas kernels  61 us (92%)
  local copies, waits for them, and re-layouts  3.21 us (5%)
  other arithmetic  1.6 us (2%)
    pallas_call x1, Pallas kernels, local(): pl.pallas_call(kernel, out_shape=(jax.ShapeDtypeStruct((1024, 512), jnp.f...  61 us
    unnamed x5, local copies, waits for them, and re-layouts  3.21 us
    div x1, other arithmetic, local(): return nodes * inflated / totals  1.6 us

profile of v1, /device:TPU:1, one launch (start us, length us, event | category | flops | bytes accessed | tf_op | source)
XLA Modules:
  0.0 65.8 jit_solution(11708132875714889870)
XLA Ops:
  0.0 0.8 %copy.4.pattern_ref = s32[4,2]{1,0:T(4,128)S(1)} copy(s32[4,2]{0,1:T(2,128)} %param.5) | data formatting | bytes 64 | tf_op args[2]
  0.8 0.0 copy-start
  0.8 1.2 %copy-done = bf16[1024,512]{1,0:T(8,128)(2,1)S(1)} copy-done((bf16[1024,512]{1,0:T(8,128)(2,1)S(1)}, bf16[1024,512]{1,0:T(8,128)(2,1)}, u32[]{:S(2)}) %copy-start) | copy-done | bytes 1048600
  2.0 0.0 copy-start.1
  2.0 1.2 %copy-done.1 = bf16[1024,512]{1,0:T(8,128)(2,1)S(1)} copy-done((bf16[1024,512]{1,0:T(8,128)(2,1)S(1)}, bf16[1024,512]{1,0:T(8,128)(2,1)}, u32[]{:S(2)}) %copy-start.1) | copy-done | bytes 1048600
  3.2 61.0 %shard_map.37 = (f32[1024,512]{1,0:T(8,128)S(1)}, f32[1,512]{1,0:T(1,128)S(1)}) custom-call(s32[4,2]{1,0:T(4,128)S(1)} %copy.4.pattern_ref, bf16[1024,512]{1,0:T(8,128)(2,1)S(1)} %copy-done, bf16[4,256,512]{2,1,0:T(8,128)(2,1)S(1)} %bitcast.3), custom_call_target="tpu_custom_call" | custom-call | flops 8589934592 | bytes 4194304 | tf_op jit(solution)/shard_map/pallas_call | solution.py:339
  64.2 1.6 %multiply_divide_fusion = f32[1024,512]{1,0:T(8,128)} fusion(f32[1024,512]{1,0:T(8,128)S(1)} %get-tuple-element.7, f32[512]{0:T(512)S(1)} %bitcast.2), kind=kLoop, calls=%fused_computation | loop fusion | flops 1048576 | bytes 4196352 | tf_op jit(solution)/shard_map/div | solution.py:383
Async XLA Ops:
  0.8 1.2 %copy-start = (bf16[1024,512]{1,0:T(8,128)(2,1)S(1)}, bf16[1024,512]{1,0:T(8,128)(2,1)}, u32[]{:S(2)}) copy-start(bf16[1024,512]{1,0:T(8,128)(2,1)} %weights_ref.1) | copy-start | bytes 3145732
  2.0 1.2 %copy-start.1 = (bf16[1024,512]{1,0:T(8,128)(2,1)S(1)}, bf16[1024,512]{1,0:T(8,128)(2,1)}, u32[]{:S(2)}) copy-start(bf16[1024,512]{1,0:T(8,128)(2,1)} %param.4) | copy-start | bytes 3145732

commit v2 on v1

v2 whole, which is shorter than its diff:
```python
import functools

import jax
import jax.numpy as jnp
from jax import lax
from jax.experimental import pallas as pl
from jax.experimental.pallas import tpu as pltpu
from jax.sharding import PartitionSpec as P

TILE = 256
MESH = pl.DeviceIdType.MESH
SIDE = 4
SLOTS = 4
COMPUTE = True

TREE = (
    ((1, 0), (0, 0)),
    ((-1, 0), (0, 0)),
    ((0, 1), (0, 0)),
    ((0, -1), (0, 0)),
    ((1, 1), (1, 0)),
    ((-1, -1), (-1, 0)),
    ((-1, 1), (0, 1)),
    ((1, -1), (0, -1)),
    ((2, 1), (1, 1)),
    ((1, 2), (1, 1)),
    ((-1, 2), (-1, 1)),
    ((2, -1), (1, -1)),
    ((2, 0), (1, 0)),
    ((0, 2), (0, 1)),
    ((2, 2), (2, 1)),
)
ROUNDS = len(TREE)
LAG = 4
STEPS = 6
UP = (0, 1, 2, 3, 0, 1)
DOWN = (2, 3, 0, 1, 2, 3)


for number, (_, parent) in enumerate(TREE):
    assert parent == (0, 0) or [o for o, _ in TREE].index(parent) <= number - LAG


def turn(offset, times):
    dx, dz = offset
    for _ in range(times):
        dx, dz = -dz, dx
    return dx, dz


def handled(step):
    return 2 * step + 1


def compute_plan():
    arrive = {(0, 0): 2}
    for number, (offset, _) in enumerate(TREE):
        for s in range(SLOTS):
            dx, dz = turn(offset, s)
            key = (dx % SIDE, dz % SIDE)
            arrive[key] = max(arrive.get(key, 0), number + 1 + LAG)
    last = ROUNDS + LAG
    orders = {}
    ready = {}
    for delta in range(SIDE):
        for parity in range(2):
            when = {}
            for (dx, dz), t in arrive.items():
                dy = (delta - dz) % SIDE
                quarter = (parity + dx) % 2
                if dy == 0:
                    b = 3
                elif dy == 2:
                    b = handled(6) + 1
                elif dy == 3:
                    b = handled(2 if quarter == 0 else 4) + 1
                else:
                    b = handled(2 if quarter == 1 else 4) + 1
                when[(dx, dz)] = max(t, b)
            order = sorted(when, key=lambda o: (when[o], o))
            orders[delta, parity] = order
            ready[delta, parity] = [when[o] for o in order]
    counts = {}
    done = 0
    for t in range(LAG + 1, last + 1):
        able = min(sum(1 for w in ready[v] if w <= t) for v in ready) - done
        take = able if t > ROUNDS else min(able, 2)
        counts[t] = take
        done += take
    assert done == SIDE * SIDE
    return orders, counts


ORDERS, COUNTS = compute_plan()


def kernel(
    pattern_ref, weights_ref, panel_ref, total, sums_ref,
    own, graph, panel, pattern, meta, part, parts, local_sem,
    a_send, a_recv, b_send, b_recv, c_send, c_recv, m_send, m_recv, t_send, t_recv,
):
    row, col = lax.axis_index("row"), lax.axis_index("col")
    y, core = row // 2, row % 2
    z, x = col // SIDE, col % SIDE

    def wrap(v):
        return (v + 2 * SIDE) % SIDE

    def at(dx, dz):
        return wrap(z + dz) * SIDE + wrap(x + dx)

    def lane(dy):
        return wrap(y + dy) * 2 + core

    other = y * 2 + 1 - core

    load_a = pltpu.make_async_copy(weights_ref, own, local_sem.at[0])
    load_p = pltpu.make_async_copy(pattern_ref, pattern, local_sem.at[1])
    mine = pl.multiple_of(row * 4, 4)
    load_b = pltpu.make_async_copy(panel_ref, panel.at[pl.ds(mine, 4)], local_sem.at[2])
    load_p.start()
    load_a.start()

    barrier = pltpu.get_barrier_semaphore()
    for peer in (
        (row, at(1, 0)), (row, at(-1, 0)), (row, at(0, 1)), (row, at(0, -1)),
        (lane(1), col), (lane(-1), col), (other, col),
    ):
        pl.semaphore_signal(barrier, inc=1, device_id=peer, device_id_type=MESH)

    load_b.start()

    load_p.wait()
    load_a.wait()
    bits = [pattern[i % 2, i // 2] for i in range(8)]
    meta[col, 0] = functools.reduce(lambda a, b: a + b, [bits[i] << i for i in range(8)])
    ranks = [jnp.int32(0)]
    for i in range(7):
        ranks.append(ranks[-1] + bits[i])

    def pack(s):
        tile = jnp.zeros((TILE, TILE), jnp.bfloat16)
        for i in range(s, 8):
            r, c = i // 2 * TILE, i % 2 * TILE
            tile = jnp.where((bits[i] == 1) & (ranks[i] == s), own[r:r + TILE, c:c + TILE], tile)
        graph[col, s] = tile

    def remote(source, target, send_sem, recv_sem, device):
        return pltpu.make_async_remote_copy(
            src_ref=source, dst_ref=target, send_sem=send_sem, recv_sem=recv_sem,
            device_id=device, device_id_type=MESH)

    def arrived(block, recv_sem):
        remote(block, block, recv_sem, recv_sem, (row, col)).wait_recv()

    def sent(block, send_sem):
        remote(block, block, send_sem, send_sem, (row, col)).wait_send()

    def a_copy(number, s):
        offset, parent = TREE[number]
        px, pz = turn(parent, s)
        dx, dz = turn((offset[0] - parent[0], offset[1] - parent[1]), s)
        tile = graph.at[at(-px, -pz), s]
        return remote(tile, tile, a_send, a_recv.at[number], (row, at(dx, dz)))

    def m_copy(number):
        offset, (px, pz) = TREE[number]
        code = meta.at[at(-px, -pz)]
        return remote(code, code, m_send, m_recv.at[number], (row, at(offset[0] - px, offset[1] - pz)))

    def a_wait(number):
        arrived(graph.at[col], a_recv.at[number])
        arrived(meta.at[col], m_recv.at[number])

    def b_copy(way, step):
        j = (UP if way > 0 else DOWN)[step - 1]
        piece = panel.at[lane(-way if step > 4 else 0) * 4 + j]
        return remote(piece, piece, b_send, b_recv.at[step - 1], (lane(way), col))

    def b_wait(step):
        arrived(panel.at[pl.ds(0, 2)], b_recv.at[step - 1])

    def c_copy(step, n):
        if step == 0:
            piece = panel.at[row * 4 + n]
        else:
            way = 1 if n == 0 else -1
            j = (UP if way > 0 else DOWN)[step - 1]
            piece = panel.at[lane(-way * (2 if step > 4 else 1)) * 4 + j]
        return remote(piece, piece, c_send, c_recv.at[step], (other, col))

    def c_range(step):
        return range(4 if step == 0 else 2)

    def c_wait(step):
        arrived(panel.at[pl.ds(0, len(c_range(step)))], c_recv.at[step])

    def ordered(place):
        index = jnp.int32(0)
        variant = wrap(z - y) * 2 + x % 2
        for v in range(8):
            dx, dz = ORDERS[v // 2, v % 2][place]
            index = jnp.where(variant == v, at(-dx, -dz), index)
        return index

    def add_source(source, first, last=False):
        sums = jnp.zeros((1, 512), jnp.float32)
        present = meta[source, 0]
        have = [(present >> i) & 1 for i in range(8)]
        before = [jnp.int32(0)]
        for i in range(7):
            before.append(before[-1] + have[i])
        tiles = [graph.at[source, s] for s in range(SLOTS)]
        piece = pl.multiple_of(source * 2, 2)
        for r in range(4):
            sides = []
            for c in range(2):
                i = 2 * r + c
                tile = jnp.zeros((TILE, TILE), jnp.bfloat16)
                for s in range(min(i + 1, SLOTS)):
                    tile = jnp.where((have[i] == 1) & (before[i] == s), tiles[s][...], tile)
                sides.append(tile)
            product = jnp.dot(sides[0], panel[piece], preferred_element_type=jnp.float32)
            product += jnp.dot(sides[1], panel[piece + 1], preferred_element_type=jnp.float32)
            rows = pl.ds(r * TILE, TILE)
            if last:
                product += total[rows, :]
                product *= product
                sums += jnp.sum(product, axis=0, keepdims=True)
                total[rows, :] = product
            elif first:
                total[rows, :] = product
            else:
                total[rows, :] += product
        return sums

    for s in range(SLOTS):
        pack(s)
        if s == 0:
            pl.semaphore_wait(barrier, 7)
        for number in range(4):
            a_copy(number, s).start()
    for number in range(4):
        m_copy(number).start()
    load_b.wait()
    for step in (1, 2):
        for way in (1, -1):
            b_copy(way, step).start()
    for n in c_range(0):
        c_copy(0, n).start()

    done = 0
    for t in range(LAG + 1, ROUNDS + LAG + 1):
        a_wait(t - LAG - 1)
        if t <= ROUNDS:
            for s in range(SLOTS):
                a_copy(t - 1, s).start()
            m_copy(t - 1).start()
        if t == LAG + 1:
            c_wait(0)
        for step in range(1, STEPS + 1):
            if t == max(handled(step), LAG + 1):
                b_wait(step)
                for n in c_range(step):
                    c_copy(step, n).start()
                if step + 2 <= STEPS:
                    for way in (1, -1):
                        b_copy(way, step + 2).start()
            if t == max(handled(step), LAG + 1) + 1:
                c_wait(step)
        for _ in range(COUNTS[t]):
            if COMPUTE and done < SIDE * SIDE - 1:
                add_source(ordered(done), done == 0)
            done += 1

    sums = add_source(ordered(done - 1), False, True)
    part[...] = sums
    for i in range(1, 8):
        remote(part, parts.at[row], t_send, t_recv, ((row + i) % 8, col)).start()
    parts[row] = sums

    sent(graph.at[pl.ds(0, ROUNDS)], a_send)
    sent(meta.at[pl.ds(0, ROUNDS)], m_send)
    sent(panel.at[pl.ds(0, 2 * STEPS)], b_send)
    sent(panel.at[pl.ds(0, 4 + 2 * STEPS)], c_send)

    arrived(parts.at[pl.ds(0, 7)], t_recv)
    whole = parts[0]
    for i in range(1, 8):
        whole += parts[i]
    sums_ref[...] = whole
    sent(parts.at[pl.ds(0, 7)], t_send)


def local(weights, panel, pattern):
    def stay(array):
        return pltpu.with_memory_space_constraint(array, pltpu.HBM)

    inflated, totals = pl.pallas_call(
        kernel,
        out_shape=(
            pltpu.VMEM((1024, 512), jnp.float32),
            pltpu.VMEM((1, 512), jnp.float32),
        ),
        in_specs=[pl.BlockSpec(memory_space=pltpu.HBM)] * 3,
        out_specs=(
            pl.BlockSpec(memory_space=pltpu.VMEM),
            pl.BlockSpec(memory_space=pltpu.VMEM),
        ),
        scratch_shapes=[
            pltpu.VMEM((1024, 512), jnp.bfloat16),
            pltpu.VMEM((16, SLOTS, TILE, TILE), jnp.bfloat16),
            pltpu.VMEM((32, TILE, 512), jnp.bfloat16),
            pltpu.SMEM((2, 4), jnp.int32),
            pltpu.SMEM((16, 128), jnp.int32),
            pltpu.VMEM((1, 512), jnp.float32),
            pltpu.VMEM((8, 1, 512), jnp.float32),
            pltpu.SemaphoreType.DMA((3,)),
            pltpu.SemaphoreType.DMA,
            pltpu.SemaphoreType.DMA((ROUNDS,)),
            pltpu.SemaphoreType.DMA,
            pltpu.SemaphoreType.DMA((STEPS,)),
            pltpu.SemaphoreType.DMA,
            pltpu.SemaphoreType.DMA((STEPS + 1,)),
            pltpu.SemaphoreType.DMA,
            pltpu.SemaphoreType.DMA((ROUNDS,)),
            pltpu.SemaphoreType.DMA,
            pltpu.SemaphoreType.DMA,
        ],
        compiler_params=pltpu.CompilerParams(
            collective_id=0, has_side_effects=True, vmem_limit_bytes=40 * 1024 * 1024
        ),
        cost_estimate=pl.CostEstimate(
            flops=2 * 1024 * 8192 * 512, bytes_accessed=4 * 1024 * 1024, transcendentals=0
        ),
    )(stay(pattern.T), stay(weights), stay(panel.reshape(4, TILE, 512)))
    nodes = jnp.float32(8192)
    return nodes * inflated / totals


def solution(mesh):
    spec = P("row", "col")
    return jax.shard_map(local, mesh=mesh, in_specs=(spec, spec, spec), out_specs=spec, check_vma=False)
```

time: 66 us -> 60.9 us (0.923)
  local copies, waits for them, and re-layouts: 3.21 us -> 0 us
  Pallas kernels: 61 us -> 59.2 us
    unnamed x5 -> x0, local copies, waits for them, and re-layouts: 3.21 us -> none
    pallas_call x1, Pallas kernels: 61 us -> 59.2 us  [local(): pl.pallas_call(kernel, out_shape=(pltpu.VMEM((1024, 512), jnp.float32), p...]
where the time goes in v2:
time: 60.9 us; the launch traced here: 60.8 us
  Pallas kernels  59.2 us (97%)
  other arithmetic  1.62 us (3%)
    pallas_call x1, Pallas kernels, local(): pl.pallas_call(kernel, out_shape=(pltpu.VMEM((1024, 512), jnp.float32), p...  59.2 us
    div x1, other arithmetic, local(): return nodes * inflated / totals  1.62 us

profile of v2, /device:TPU:1, one launch (start us, length us, event | category | flops | bytes accessed | tf_op | source)
XLA Modules:
  0.0 60.8 jit_solution(12496777886186713217)
XLA Ops:
  0.0 59.2 %shard_map.37 = (f32[1024,512]{1,0:T(8,128)S(1)}, f32[1,512]{1,0:T(1,128)S(1)}) custom-call(s32[2,4]{1,0:T(2,128)} %bitcast.5, bf16[1024,512]{1,0:T(8,128)(2,1)} %weights_ref.1, bf16[4,256,512]{2,1,0:T(8,128)(2,1)} %bitcast.4), custom_call_target="tpu_custom_call" | custom-call | flops 8589934592 | bytes 4194304 | tf_op jit(solution)/shard_map/pallas_call | solution.py:299
  59.2 1.6 %multiply_divide_fusion = f32[1024,512]{1,0:T(8,128)} fusion(f32[1024,512]{1,0:T(8,128)S(1)} %get-tuple-element.7, f32[512]{0:T(512)S(1)} %bitcast.3), kind=kLoop, calls=%fused_computation | loop fusion | flops 1048576 | bytes 4196352 | tf_op jit(solution)/shard_map/div | solution.py:338

commit v3 on v2

v3 whole, which is shorter than its diff:
```python
import functools

import jax
import jax.numpy as jnp
from jax import lax
from jax.experimental import pallas as pl
from jax.experimental.pallas import tpu as pltpu
from jax.sharding import PartitionSpec as P

TILE = 256
MESH = pl.DeviceIdType.MESH
SIDE = 4
SLOTS = 4
STEPS = 3
UP = (0, 2, 0)
DOWN = (2, 0, 2)


def turn(offset, times):
    dx, dz = offset
    for _ in range(times):
        dx, dz = -dz, dx
    return dx, dz


def around(offset, parent, first):
    return [(turn(offset, k), turn(parent, k), first, 2) for k in range(4)]


PHASES = (
    around((1, 0), (0, 0), 0),
    around((1, 0), (0, 0), 2),
    around((1, 1), (1, 0), 0),
    around((1, 1), (1, 0), 2),
    around((2, 1), (1, 1), 0),
    around((2, 1), (1, 1), 2),
    [((2, 0), (1, 0), 0, 2), ((2, 0), (-1, 0), 2, 2), ((0, 2), (0, 1), 0, 2), ((0, 2), (0, -1), 2, 2)],
    [((2, 2), (2, 1), 0, 1), ((2, 2), (2, -1), 1, 1), ((2, 2), (1, 2), 2, 1), ((2, 2), (-1, 2), 3, 1)],
)
CODES = {
    1: [leg[:2] for leg in PHASES[1]],
    3: [leg[:2] for leg in PHASES[3]],
    5: [leg[:2] for leg in PHASES[5]],
    6: [((2, 0), (1, 0)), ((0, 2), (0, 1))],
    7: [((2, 2), (2, 1))],
}
MOMENTS = (
    ("a", 0), ("c", 0), ("a", 1), ("b", 1), ("a", 2), ("c", 1), ("a", 3), ("b", 2),
    ("a", 4), ("c", 2), ("a", 5), ("b", 3), ("c", 3), ("a", 6), ("a", 7),
)


def compute_plan():
    when = {moment: i for i, moment in enumerate(MOMENTS)}
    arrive = {(0, 0): 0}
    for number, legs in enumerate(PHASES):
        for (dx, dz), _, _, _ in legs:
            arrive[dx % SIDE, dz % SIDE] = when["a", number]
    orders, ready = {}, {}
    for delta in range(SIDE):
        for parity in range(2):
            able = {}
            for (dx, dz), moment in arrive.items():
                dy = (delta - dz) % SIDE
                quarter = (parity + dx) % 2
                step = {0: 0, 2: 3, 3: 1 + quarter, 1: 2 - quarter}[dy]
                able[dx, dz] = max(moment, when["c", step])
            order = sorted(able, key=lambda o: (able[o], o))
            orders[delta, parity] = order
            ready[delta, parity] = [able[o] for o in order]
    counts, done = [], 0
    for i in range(len(MOMENTS)):
        take = min(sum(1 for w in ready[v] if w <= i) for v in ready) - done
        counts.append(take)
        done += take
    assert done == SIDE * SIDE and counts[-1] == 1
    return orders, counts


ORDERS, COUNTS = compute_plan()


def kernel(
    pattern_ref, weights_ref, panel_ref, total, sums_ref,
    own, graph, panel, pattern, meta, part, parts, local_sem,
    a_send, a_recv, b_send, b_recv, c_send, c_recv, m_send, m_recv, t_send, t_recv,
):
    row, col = lax.axis_index("row"), lax.axis_index("col")
    y, core = row // 2, row % 2
    z, x = col // SIDE, col % SIDE

    def wrap(v):
        return (v + 2 * SIDE) % SIDE

    def at(dx, dz):
        return wrap(z + dz) * SIDE + wrap(x + dx)

    def lane(dy):
        return wrap(y + dy) * 2 + core

    other = y * 2 + 1 - core

    load_p = pltpu.make_async_copy(pattern_ref, pattern, local_sem.at[1])
    mine = pl.multiple_of(row * 4, 4)
    load_b = pltpu.make_async_copy(panel_ref, panel.at[pl.ds(mine, 4)], local_sem.at[2])
    load_p.start()
    for i in range(4):
        rows = pl.ds(i * TILE, TILE)
        pltpu.make_async_copy(weights_ref.at[rows], own.at[rows], local_sem.at[0]).start()

    barrier = pltpu.get_barrier_semaphore()
    for peer in (
        (row, at(1, 0)), (row, at(-1, 0)), (row, at(0, 1)), (row, at(0, -1)),
        (lane(1), col), (lane(-1), col), (other, col),
    ):
        pl.semaphore_signal(barrier, inc=1, device_id=peer, device_id_type=MESH)


    load_p.wait()
    pltpu.make_async_copy(weights_ref, own, local_sem.at[0]).wait()
    load_b.start()
    bits = [pattern[i % 2, i // 2] for i in range(8)]
    meta[col, 0] = functools.reduce(lambda a, b: a + b, [bits[i] << i for i in range(8)])
    ranks = [jnp.int32(0)]
    for i in range(7):
        ranks.append(ranks[-1] + bits[i])

    def pack(s):
        tile = jnp.zeros((TILE, TILE), jnp.bfloat16)
        for i in range(s, 8):
            r, c = i // 2 * TILE, i % 2 * TILE
            tile = jnp.where((bits[i] == 1) & (ranks[i] == s), own[r:r + TILE, c:c + TILE], tile)
        graph[col, s] = tile

    def remote(source, target, send_sem, recv_sem, device):
        return pltpu.make_async_remote_copy(
            src_ref=source, dst_ref=target, send_sem=send_sem, recv_sem=recv_sem,
            device_id=device, device_id_type=MESH)

    def arrived(block, recv_sem):
        remote(block, block, recv_sem, recv_sem, (row, col)).wait_recv()

    def sent(block, send_sem):
        remote(block, block, send_sem, send_sem, (row, col)).wait_send()

    def send(number):
        for (dx, dz), (px, pz), first, count in PHASES[number]:
            tiles = graph.at[at(-px, -pz), pl.ds(first, count)]
            remote(tiles, tiles, a_send, a_recv.at[number], (row, at(dx - px, dz - pz))).start()

    def send_codes(number):
        for (dx, dz), (px, pz) in CODES[number]:
            code = meta.at[at(-px, -pz)]
            remote(code, code, m_send, m_recv.at[number], (row, at(dx - px, dz - pz))).start()

    def a_wait(number):
        count = sum(leg[3] for leg in PHASES[number]) // SLOTS
        arrived(graph.at[pl.ds(0, count)], a_recv.at[number])
        if number in CODES:
            arrived(meta.at[pl.ds(0, len(CODES[number]))], m_recv.at[number])

    def two(device_row, j):
        return panel.at[pl.ds(device_row * 4 + j, 2)]

    def b_copy(way, step):
        pieces = two(lane(-way if step == STEPS else 0), (UP if way > 0 else DOWN)[step - 1])
        return remote(pieces, pieces, b_send, b_recv.at[step - 1], (lane(way), col))

    def b_wait(step):
        arrived(panel.at[pl.ds(0, 4)], b_recv.at[step - 1])

    def c_copy(step, way):
        if step == 0:
            pieces = panel.at[pl.ds(mine, 4)]
        else:
            hops = 2 if step == STEPS else 1
            pieces = two(lane(-way * hops), (UP if way > 0 else DOWN)[step - 1])
        return remote(pieces, pieces, c_send, c_recv.at[step], (other, col))

    def c_wait(step):
        arrived(panel.at[pl.ds(0, 4)], c_recv.at[step])

    def ordered(place):
        index = jnp.int32(0)
        variant = wrap(z - y) * 2 + x % 2
        for v in range(8):
            dx, dz = ORDERS[v // 2, v % 2][place]
            index = jnp.where(variant == v, at(-dx, -dz), index)
        return index

    def add_source(source, first, last=False):
        sums = jnp.zeros((1, 512), jnp.float32)
        present = meta[source, 0]
        have = [(present >> i) & 1 for i in range(8)]
        before = [jnp.int32(0)]
        for i in range(7):
            before.append(before[-1] + have[i])
        tiles = [graph.at[source, s] for s in range(SLOTS)]
        piece = pl.multiple_of(source * 2, 2)
        for r in range(4):
            sides = []
            for c in range(2):
                i = 2 * r + c
                tile = jnp.zeros((TILE, TILE), jnp.bfloat16)
                for s in range(min(i + 1, SLOTS)):
                    tile = jnp.where((have[i] == 1) & (before[i] == s), tiles[s][...], tile)
                sides.append(tile)
            product = jnp.dot(sides[0], panel[piece], preferred_element_type=jnp.float32)
            product += jnp.dot(sides[1], panel[piece + 1], preferred_element_type=jnp.float32)
            rows = pl.ds(r * TILE, TILE)
            if last:
                product += total[rows, :]
                product *= product
                sums += jnp.sum(product, axis=0, keepdims=True)
                total[rows, :] = product
            elif first:
                total[rows, :] = product
            else:
                total[rows, :] += product
        return sums

    pack(0)
    pack(1)
    pl.semaphore_wait(barrier, 7)
    send(0)
    pack(2)
    pack(3)
    send(1)
    send_codes(1)
    load_b.wait()
    for step in (1, 2):
        for way in (1, -1):
            b_copy(way, step).start()
    c_copy(0, 1).start()

    done = 0
    for (kind, number), count in zip(MOMENTS, COUNTS):
        if kind == "a":
            a_wait(number)
            for later in {0: (2,), 1: (3,), 2: (4,), 3: (5, 6), 5: (7,)}.get(number, ()):
                send(later)
                if later in CODES:
                    send_codes(later)
        elif kind == "b":
            b_wait(number)
            for way in (1, -1):
                c_copy(number, way).start()
            if number + 2 <= STEPS:
                for way in (1, -1):
                    b_copy(way, number + 2).start()
        else:
            c_wait(number)
        for _ in range(count):
            if done < SIDE * SIDE - 1:
                add_source(ordered(done), done == 0)
            done += 1

    sums = add_source(ordered(done - 1), False, True)
    part[...] = sums
    for i in range(1, 8):
        remote(part, parts.at[row], t_send, t_recv, ((row + i) % 8, col)).start()
    parts[row] = sums

    sent(graph.at[pl.ds(0, 15)], a_send)
    sent(meta.at[pl.ds(0, 15)], m_send)
    sent(panel.at[pl.ds(0, 4 * STEPS)], b_send)
    sent(panel.at[pl.ds(0, 4 + 4 * STEPS)], c_send)

    arrived(parts.at[pl.ds(0, 7)], t_recv)
    whole = parts[0]
    for i in range(1, 8):
        whole += parts[i]
    sums_ref[...] = whole
    sent(parts.at[pl.ds(0, 7)], t_send)


def divide(inflated_ref, totals_ref, flow_ref, held, sem):
    size = 1024 // 8
    for i in range(8):
        rows = pl.ds(i * size, size)
        held[rows, :] = jnp.float32(8192) * inflated_ref[rows, :] / totals_ref[...]
        pltpu.make_async_copy(held.at[rows], flow_ref.at[rows], sem).start()
    pltpu.make_async_copy(held, flow_ref, sem).wait()


def local(weights, panel, pattern):
    def stay(array):
        return pltpu.with_memory_space_constraint(array, pltpu.HBM)

    inflated, totals = pl.pallas_call(
        kernel,
        out_shape=(
            pltpu.VMEM((1024, 512), jnp.float32),
            pltpu.VMEM((1, 512), jnp.float32),
        ),
        in_specs=[pl.BlockSpec(memory_space=pltpu.HBM)] * 3,
        out_specs=(
            pl.BlockSpec(memory_space=pltpu.VMEM),
            pl.BlockSpec(memory_space=pltpu.VMEM),
        ),
        scratch_shapes=[
            pltpu.VMEM((1024, 512), jnp.bfloat16),
            pltpu.VMEM((16, SLOTS, TILE, TILE), jnp.bfloat16),
            pltpu.VMEM((32, TILE, 512), jnp.bfloat16),
            pltpu.SMEM((2, 4), jnp.int32),
            pltpu.SMEM((16, 128), jnp.int32),
            pltpu.VMEM((1, 512), jnp.float32),
            pltpu.VMEM((8, 1, 512), jnp.float32),
            pltpu.SemaphoreType.DMA((3,)),
            pltpu.SemaphoreType.DMA,
            pltpu.SemaphoreType.DMA((len(PHASES),)),
            pltpu.SemaphoreType.DMA,
            pltpu.SemaphoreType.DMA((STEPS,)),
            pltpu.SemaphoreType.DMA,
            pltpu.SemaphoreType.DMA((STEPS + 1,)),
            pltpu.SemaphoreType.DMA,
            pltpu.SemaphoreType.DMA((len(PHASES),)),
            pltpu.SemaphoreType.DMA,
            pltpu.SemaphoreType.DMA,
        ],
        compiler_params=pltpu.CompilerParams(
            collective_id=0, has_side_effects=True, vmem_limit_bytes=40 * 1024 * 1024
        ),
        cost_estimate=pl.CostEstimate(
            flops=2 * 1024 * 8192 * 512, bytes_accessed=4 * 1024 * 1024, transcendentals=0
        ),
    )(stay(pattern.T), stay(weights), stay(panel.reshape(4, TILE, 512)))
    return pl.pallas_call(
        divide,
        out_shape=jax.ShapeDtypeStruct((1024, 512), jnp.float32),
        in_specs=[pl.BlockSpec(memory_space=pltpu.VMEM)] * 2,
        out_specs=pl.BlockSpec(memory_space=pltpu.HBM),
        scratch_shapes=[pltpu.VMEM((1024, 512), jnp.float32), pltpu.SemaphoreType.DMA],
        compiler_params=pltpu.CompilerParams(vmem_limit_bytes=16 * 1024 * 1024),
    )(
        pltpu.with_memory_space_constraint(inflated, pltpu.VMEM),
        pltpu.with_memory_space_constraint(totals, pltpu.VMEM),
    )


def solution(mesh):
    spec = P("row", "col")
    return jax.shard_map(local, mesh=mesh, in_specs=(spec, spec, spec), out_specs=spec, check_vma=False)
```

time: 60.9 us -> 58.1 us (0.954)
  other arithmetic: 1.62 us -> 0 us
  Pallas kernels: 59.2 us -> 58 us
    pallas_call x1, Pallas kernels: 59.2 us -> 56.7 us  [local(): pl.pallas_call(kernel, out_shape=(pltpu.VMEM((1024, 512), jnp.float32), p...]
    div x1 -> x0, other arithmetic: 1.62 us -> none  [local(): return nodes * inflated / totals]
    pallas_call x0 -> x1, Pallas kernels: none -> 1.34 us  [local(): pl.pallas_call(divide, out_shape=jax.ShapeDtypeStruct((1024, 512), jnp.fl...]
where the time goes in v3:
time: 58.1 us; the launch traced here: 58 us
  Pallas kernels  58 us (100%)
    pallas_call x1, Pallas kernels, local(): pl.pallas_call(kernel, out_shape=(pltpu.VMEM((1024, 512), jnp.float32), p...  56.7 us
    pallas_call x1, Pallas kernels, local(): pl.pallas_call(divide, out_shape=jax.ShapeDtypeStruct((1024, 512), jnp.fl...  1.34 us

profile of v3, /device:TPU:1, one launch (start us, length us, event | category | flops | bytes accessed | tf_op | source)
XLA Modules:
  0.0 58.0 jit_solution(5122868449052801057)
XLA Ops:
  0.0 56.7 %shard_map.37 = (f32[1024,512]{1,0:T(8,128)S(1)}, f32[1,512]{1,0:T(1,128)S(1)}) custom-call(s32[2,4]{1,0:T(2,128)} %bitcast.3, bf16[1024,512]{1,0:T(8,128)(2,1)} %weights_ref.1, bf16[4,256,512]{2,1,0:T(8,128)(2,1)} %bitcast.2), custom_call_target="tpu_custom_call" | custom-call | flops 8589934592 | bytes 4194304 | tf_op jit(solution)/shard_map/pallas_call | solution.py:290
  56.7 1.3 %shard_map.38 = f32[1024,512]{1,0:T(8,128)} custom-call(f32[1024,512]{1,0:T(8,128)S(1)} %get-tuple-element.7.inflated_ref, f32[1,512]{1,0:T(1,128)S(1)} %get-tuple-element.8.totals_ref), custom_call_target="tpu_custom_call" | custom-call | tf_op jit(solution)/shard_map/pallas_call | solution.py:328

commit v4 on v3

--- a/solution.py
+++ b/solution.py
@@ -8,6 +8,7 @@
 from jax.sharding import PartitionSpec as P
 
 TILE = 256
+HALF = 128
 MESH = pl.DeviceIdType.MESH
 SIDE = 4
 SLOTS = 4
@@ -35,6 +36,7 @@
     around((2, 1), (1, 1), 0),
     around((2, 1), (1, 1), 2),
     [((2, 0), (1, 0), 0, 2), ((2, 0), (-1, 0), 2, 2), ((0, 2), (0, 1), 0, 2), ((0, 2), (0, -1), 2, 2)],
+    [((2, 2), (2, 1), 0, 1), ((2, 2), (2, -1), 1, 1), ((2, 2), (1, 2), 2, 1), ((2, 2), (-1, 2), 3, 1)],
     [((2, 2), (2, 1), 0, 1), ((2, 2), (2, -1), 1, 1), ((2, 2), (1, 2), 2, 1), ((2, 2), (-1, 2), 3, 1)],
 )
 CODES = {
@@ -46,7 +48,7 @@
 }
 MOMENTS = (
     ("a", 0), ("c", 0), ("a", 1), ("b", 1), ("a", 2), ("c", 1), ("a", 3), ("b", 2),
-    ("a", 4), ("c", 2), ("a", 5), ("b", 3), ("c", 3), ("a", 6), ("a", 7),
+    ("a", 4), ("c", 2), ("a", 5), ("b", 3), ("c", 3), ("a", 6), ("a", 7), ("a", 8),
 )
 
 
@@ -83,7 +85,7 @@
 def kernel(
     pattern_ref, weights_ref, panel_ref, total, sums_ref,
     own, graph, panel, pattern, meta, part, parts, local_sem,
-    a_send, a_recv, b_send, b_recv, c_send, c_recv, m_send, m_recv, t_send, t_recv,
+    a_send, a_recv, b_send, b_recv, c_send, c_recv, m_send, m_recv, t_send, t_recv, both,
 ):
     row, col = lax.axis_index("row"), lax.axis_index("col")
     y, core = row // 2, row % 2
@@ -97,6 +99,9 @@
 
     def lane(dy):
         return wrap(y + dy) * 2 + core
+
+    def lane_of(dy, which):
+        return wrap(y + dy) * 2 + which
 
     other = y * 2 + 1 - core
 
@@ -109,28 +114,36 @@
         pltpu.make_async_copy(weights_ref.at[rows], own.at[rows], local_sem.at[0]).start()
 
     barrier = pltpu.get_barrier_semaphore()
-    for peer in (
-        (row, at(1, 0)), (row, at(-1, 0)), (row, at(0, 1)), (row, at(0, -1)),
-        (lane(1), col), (lane(-1), col), (other, col),
-    ):
-        pl.semaphore_signal(barrier, inc=1, device_id=peer, device_id_type=MESH)
-
+    for sign in (1, -1):
+        for peer in (
+            (lane_of(0, 0), at(sign, 0)), (lane_of(0, 1), at(0, sign)), (lane(sign), col),
+        ):
+            pl.semaphore_signal(barrier, inc=1, device_id=peer, device_id_type=MESH)
+    pl.semaphore_signal(barrier, inc=1, device_id=(other, col), device_id_type=MESH)
 
     load_p.wait()
     pltpu.make_async_copy(weights_ref, own, local_sem.at[0]).wait()
     load_b.start()
     bits = [pattern[i % 2, i // 2] for i in range(8)]
     meta[col, 0] = functools.reduce(lambda a, b: a + b, [bits[i] << i for i in range(8)])
-    ranks = [jnp.int32(0)]
-    for i in range(7):
-        ranks.append(ranks[-1] + bits[i])
+    def places(have):
+        gaps, extras = [jnp.int32(0)], [jnp.int32(0)]
+        for i in range(3):
+            gaps.append(gaps[-1] + 1 - have[i])
+            extras.append(extras[-1] + have[4 + i])
+        return [[(have[s] == 0) & (have[4 + i] == 1) & (gaps[s] == extras[i]) for i in range(4)] for s in range(SLOTS)]
+
+    holds = places(bits)
 
     def pack(s):
-        tile = jnp.zeros((TILE, TILE), jnp.bfloat16)
-        for i in range(s, 8):
+        def tile(i):
             r, c = i // 2 * TILE, i % 2 * TILE
-            tile = jnp.where((bits[i] == 1) & (ranks[i] == s), own[r:r + TILE, c:c + TILE], tile)
-        graph[col, s] = tile
+            return own[r:r + TILE, c:c + TILE]
+
+        packed = tile(s)
+        for i in range(4):
+            packed = jnp.where(holds[s][i], tile(4 + i), packed)
+        graph[col, s] = packed
 
     def remote(source, target, send_sem, recv_sem, device):
         return pltpu.make_async_remote_copy(
@@ -146,6 +159,8 @@
     def send(number):
         for (dx, dz), (px, pz), first, count in PHASES[number]:
             tiles = graph.at[at(-px, -pz), pl.ds(first, count)]
+            if number >= 7:
+                tiles = tiles.at[:, pl.ds((number - 7) * HALF, HALF)]
             remote(tiles, tiles, a_send, a_recv.at[number], (row, at(dx - px, dz - pz))).start()
 
     def send_codes(number):
@@ -154,8 +169,10 @@
             remote(code, code, m_send, m_recv.at[number], (row, at(dx - px, dz - pz))).start()
 
     def a_wait(number):
-        count = sum(leg[3] for leg in PHASES[number]) // SLOTS
-        arrived(graph.at[pl.ds(0, count)], a_recv.at[number])
+        if number >= 7:
+            arrived(graph.at[0, pl.ds(0, 2)], a_recv.at[number])
+        else:
+            arrived(graph.at[pl.ds(0, 2)], a_recv.at[number])
         if number in CODES:
             arrived(meta.at[pl.ds(0, len(CODES[number]))], m_recv.at[number])
 
@@ -188,44 +205,61 @@
             index = jnp.where(variant == v, at(-dx, -dz), index)
         return index
 
-    def add_source(source, first, last=False):
-        sums = jnp.zeros((1, 512), jnp.float32)
+    def product(source, have, holding, r, start, size):
+        piece = pl.multiple_of(source * 2, 2)
+        value = jnp.zeros((size, 512), jnp.float32)
+        for c in range(2):
+            i = 2 * r + c
+            tile = jnp.zeros((size, TILE), jnp.bfloat16)
+            for s in range(SLOTS) if i >= 4 else (i,):
+                taken = holding[s][i - 4] if i >= 4 else have[i] == 1
+                tile = jnp.where(taken, graph[source, s, start:start + size, :], tile)
+            value += jnp.dot(tile, panel[piece + c], preferred_element_type=jnp.float32)
+        return value
+
+    def code(source):
         present = meta[source, 0]
         have = [(present >> i) & 1 for i in range(8)]
-        before = [jnp.int32(0)]
-        for i in range(7):
-            before.append(before[-1] + have[i])
-        tiles = [graph.at[source, s] for s in range(SLOTS)]
-        piece = pl.multiple_of(source * 2, 2)
+        return have, places(have)
+
+    def add_source(source, first):
+        have, holding = code(source)
         for r in range(4):
-            sides = []
-            for c in range(2):
-                i = 2 * r + c
-                tile = jnp.zeros((TILE, TILE), jnp.bfloat16)
-                for s in range(min(i + 1, SLOTS)):
-                    tile = jnp.where((have[i] == 1) & (before[i] == s), tiles[s][...], tile)
-                sides.append(tile)
-            product = jnp.dot(sides[0], panel[piece], preferred_element_type=jnp.float32)
-            product += jnp.dot(sides[1], panel[piece + 1], preferred_element_type=jnp.float32)
             rows = pl.ds(r * TILE, TILE)
-            if last:
-                product += total[rows, :]
-                product *= product
-                sums += jnp.sum(product, axis=0, keepdims=True)
-                total[rows, :] = product
-            elif first:
-                total[rows, :] = product
+            value = product(source, have, holding, r, 0, TILE)
+            if first:
+                total[rows, :] = value
             else:
-                total[rows, :] += product
+                total[rows, :] += value
+
+    def finish(source, half):
+        have, holding = code(source)
+        sums = jnp.zeros((1, 512), jnp.float32)
+        for r in range(4):
+            rows = pl.ds(r * TILE + half * HALF, HALF)
+            value = total[rows, :] + product(source, have, holding, r, half * HALF, HALF)
+            value = value * value
+            total[rows, :] = value
+            sums += jnp.sum(value, axis=0, keepdims=True)
         return sums
+
+    def own_pair(number, along):
+        for sign in (1, -1):
+            tiles = graph.at[col, pl.ds(2 * number, 2)]
+            target = at(sign * (1 - along), sign * along)
+            remote(tiles, tiles, a_send, a_recv.at[number], (row, target)).start()
 
     pack(0)
     pack(1)
     pl.semaphore_wait(barrier, 7)
-    send(0)
+    pl.semaphore_signal(both, inc=1, device_id=(other, col), device_id_type=MESH)
+    own_pair(0, core)
     pack(2)
     pack(3)
-    send(1)
+    pl.semaphore_wait(both, 1)
+    own_pair(0, 1 - core)
+    own_pair(1, core)
+    own_pair(1, 1 - core)
     send_codes(1)
     load_b.wait()
     for step in (1, 2):
@@ -234,10 +268,11 @@
     c_copy(0, 1).start()
 
     done = 0
+    sums = []
     for (kind, number), count in zip(MOMENTS, COUNTS):
         if kind == "a":
             a_wait(number)
-            for later in {0: (2,), 1: (3,), 2: (4,), 3: (5, 6), 5: (7,)}.get(number, ()):
+            for later in {0: (2,), 1: (3,), 2: (4,), 3: (5, 6), 5: (7, 8)}.get(number, ()):
                 send(later)
                 if later in CODES:
                     send_codes(later)
@@ -254,12 +289,13 @@
             if done < SIDE * SIDE - 1:
                 add_source(ordered(done), done == 0)
             done += 1
-
-    sums = add_source(ordered(done - 1), False, True)
-    part[...] = sums
+        if kind == "a" and number >= 7:
+            sums.append(finish(ordered(SIDE * SIDE - 1), number - 7))
+
+    part[...] = sums[0] + sums[1]
     for i in range(1, 8):
         remote(part, parts.at[row], t_send, t_recv, ((row + i) % 8, col)).start()
-    parts[row] = sums
+    parts[row] = sums[0] + sums[1]
 
     sent(graph.at[pl.ds(0, 15)], a_send)
     sent(meta.at[pl.ds(0, 15)], m_send)
@@ -317,6 +353,7 @@
             pltpu.SemaphoreType.DMA((len(PHASES),)),
             pltpu.SemaphoreType.DMA,
             pltpu.SemaphoreType.DMA,
+            pltpu.SemaphoreType.REGULAR,
         ],
         compiler_params=pltpu.CompilerParams(
             collective_id=0, has_side_effects=True, vmem_limit_bytes=40 * 1024 * 1024

time: 58.1 us -> 57.1 us (0.983)
  Pallas kernels: 58 us -> 56.9 us
    pallas_call x1, Pallas kernels: 56.7 us -> 55.6 us  [local(): pl.pallas_call(kernel, out_shape=(pltpu.VMEM((1024, 512), jnp.float32), p...]
where the time goes in v4:
time: 57.1 us; the launch traced here: 57 us
  Pallas kernels  56.9 us (100%)
    pallas_call x1, Pallas kernels, local(): pl.pallas_call(kernel, out_shape=(pltpu.VMEM((1024, 512), jnp.float32), p...  55.6 us
    pallas_call x1, Pallas kernels, local(): pl.pallas_call(divide, out_shape=jax.ShapeDtypeStruct((1024, 512), jnp.fl...  1.34 us

profile of v4, /device:TPU:1, one launch (start us, length us, event | category | flops | bytes accessed | tf_op | source)
XLA Modules:
  0.0 57.0 jit_solution(12194757973486458518)
XLA Ops:
  0.0 55.6 %shard_map.37 = (f32[1024,512]{1,0:T(8,128)S(1)}, f32[1,512]{1,0:T(1,128)S(1)}) custom-call(s32[2,4]{1,0:T(2,128)} %bitcast.3, bf16[1024,512]{1,0:T(8,128)(2,1)} %weights_ref.1, bf16[4,256,512]{2,1,0:T(8,128)(2,1)} %bitcast.2), custom_call_target="tpu_custom_call" | custom-call | flops 8589934592 | bytes 4194304 | tf_op jit(solution)/shard_map/pallas_call | solution.py:326
  55.6 1.3 %shard_map.38 = f32[1024,512]{1,0:T(8,128)} custom-call(f32[1024,512]{1,0:T(8,128)S(1)} %get-tuple-element.7.inflated_ref, f32[1,512]{1,0:T(1,128)S(1)} %get-tuple-element.8.totals_ref), custom_call_target="tpu_custom_call" | custom-call | tf_op jit(solution)/shard_map/pallas_call | solution.py:365

commit v5 on v4

--- a/solution.py
+++ b/solution.py
@@ -84,7 +84,7 @@
 
 def kernel(
     pattern_ref, weights_ref, panel_ref, total, sums_ref,
-    own, graph, panel, pattern, meta, part, parts, local_sem,
+    own, left, graph, panel, pattern, meta, part, parts, local_sem,
     a_send, a_recv, b_send, b_recv, c_send, c_recv, m_send, m_recv, t_send, t_recv, both,
 ):
     row, col = lax.axis_index("row"), lax.axis_index("col")
@@ -109,9 +109,13 @@
     mine = pl.multiple_of(row * 4, 4)
     load_b = pltpu.make_async_copy(panel_ref, panel.at[pl.ds(mine, 4)], local_sem.at[2])
     load_p.start()
-    for i in range(4):
-        rows = pl.ds(i * TILE, TILE)
-        pltpu.make_async_copy(weights_ref.at[rows], own.at[rows], local_sem.at[0]).start()
+    def load_a(i, first, size):
+        rows = pl.ds(first, size)
+        return pltpu.make_async_copy(weights_ref.at[rows], own.at[rows], local_sem.at[i])
+
+    load_a(0, 512, 512).start()
+    load_a(3, 0, 256).start()
+    load_a(4, 256, 256).start()
 
     barrier = pltpu.get_barrier_semaphore()
     for sign in (1, -1):
@@ -122,8 +126,6 @@
     pl.semaphore_signal(barrier, inc=1, device_id=(other, col), device_id_type=MESH)
 
     load_p.wait()
-    pltpu.make_async_copy(weights_ref, own, local_sem.at[0]).wait()
-    load_b.start()
     bits = [pattern[i % 2, i // 2] for i in range(8)]
     meta[col, 0] = functools.reduce(lambda a, b: a + b, [bits[i] << i for i in range(8)])
     def places(have):
@@ -205,17 +207,19 @@
             index = jnp.where(variant == v, at(-dx, -dz), index)
         return index
 
-    def product(source, have, holding, r, start, size):
+    def unpacked(source, have, holding, i, start, size):
+        tile = jnp.zeros((size, TILE), jnp.bfloat16)
+        for s in range(SLOTS) if i >= 4 else (i,):
+            taken = holding[s][i - 4] if i >= 4 else have[i] == 1
+            tile = jnp.where(taken, graph[source, s, start:start + size, :], tile)
+        return tile
+
+    def product(source, have, holding, r):
         piece = pl.multiple_of(source * 2, 2)
-        value = jnp.zeros((size, 512), jnp.float32)
-        for c in range(2):
-            i = 2 * r + c
-            tile = jnp.zeros((size, TILE), jnp.bfloat16)
-            for s in range(SLOTS) if i >= 4 else (i,):
-                taken = holding[s][i - 4] if i >= 4 else have[i] == 1
-                tile = jnp.where(taken, graph[source, s, start:start + size, :], tile)
-            value += jnp.dot(tile, panel[piece + c], preferred_element_type=jnp.float32)
-        return value
+        return sum(
+            jnp.dot(unpacked(source, have, holding, 2 * r + c, 0, TILE), panel[piece + c],
+                    preferred_element_type=jnp.float32)
+            for c in range(2))
 
     def code(source):
         present = meta[source, 0]
@@ -226,7 +230,7 @@
         have, holding = code(source)
         for r in range(4):
             rows = pl.ds(r * TILE, TILE)
-            value = product(source, have, holding, r, 0, TILE)
+            value = product(source, have, holding, r)
             if first:
                 total[rows, :] = value
             else:
@@ -234,13 +238,20 @@
 
     def finish(source, half):
         have, holding = code(source)
-        sums = jnp.zeros((1, 512), jnp.float32)
+        for r in range(4):
+            for c in range(2):
+                left[r * HALF:(r + 1) * HALF, c * TILE:(c + 1) * TILE] = unpacked(
+                    source, have, holding, 2 * r + c, half * HALF, HALF)
+        piece = pl.multiple_of(source * 2, 2)
+        right = panel[pl.ds(piece, 2)].reshape(2 * TILE, 512)
+        value = jnp.dot(left[...], right, preferred_element_type=jnp.float32)
+        sums = jnp.zeros((8, 512), jnp.float32)
         for r in range(4):
             rows = pl.ds(r * TILE + half * HALF, HALF)
-            value = total[rows, :] + product(source, have, holding, r, half * HALF, HALF)
-            value = value * value
-            total[rows, :] = value
-            sums += jnp.sum(value, axis=0, keepdims=True)
+            square = total[rows, :] + value[r * HALF:(r + 1) * HALF]
+            square = square * square
+            total[rows, :] = square
+            sums += jnp.sum(square.reshape(HALF // 8, 8, 512), axis=0)
         return sums
 
     def own_pair(number, along):
@@ -249,11 +260,15 @@
             target = at(sign * (1 - along), sign * along)
             remote(tiles, tiles, a_send, a_recv.at[number], (row, target)).start()
 
+    load_a(0, 512, 512).wait()
+    load_a(3, 0, 256).wait()
     pack(0)
     pack(1)
+    load_b.start()
     pl.semaphore_wait(barrier, 7)
     pl.semaphore_signal(both, inc=1, device_id=(other, col), device_id_type=MESH)
     own_pair(0, core)
+    load_a(4, 256, 256).wait()
     pack(2)
     pack(3)
     pl.semaphore_wait(both, 1)
@@ -292,10 +307,11 @@
         if kind == "a" and number >= 7:
             sums.append(finish(ordered(SIDE * SIDE - 1), number - 7))
 
-    part[...] = sums[0] + sums[1]
+    sums = jnp.sum(sums[0] + sums[1], axis=0, keepdims=True)
+    part[...] = sums
     for i in range(1, 8):
         remote(part, parts.at[row], t_send, t_recv, ((row + i) % 8, col)).start()
-    parts[row] = sums[0] + sums[1]
+    parts[row] = sums
 
     sent(graph.at[pl.ds(0, 15)], a_send)
     sent(meta.at[pl.ds(0, 15)], m_send)
@@ -336,13 +352,14 @@
         ),
         scratch_shapes=[
             pltpu.VMEM((1024, 512), jnp.bfloat16),
+            pltpu.VMEM((4 * HALF, 2 * TILE), jnp.bfloat16),
             pltpu.VMEM((16, SLOTS, TILE, TILE), jnp.bfloat16),
             pltpu.VMEM((32, TILE, 512), jnp.bfloat16),
             pltpu.SMEM((2, 4), jnp.int32),
             pltpu.SMEM((16, 128), jnp.int32),
             pltpu.VMEM((1, 512), jnp.float32),
             pltpu.VMEM((8, 1, 512), jnp.float32),
-            pltpu.SemaphoreType.DMA((3,)),
+            pltpu.SemaphoreType.DMA((5,)),
             pltpu.SemaphoreType.DMA,
             pltpu.SemaphoreType.DMA((len(PHASES),)),
             pltpu.SemaphoreType.DMA,

time: 57.1 us -> 56.9 us (level)
  no operation moved by 1% of the time
where the time goes in v5:
time: 56.9 us; the launch traced here: 56.8 us
  Pallas kernels  56.8 us (100%)
    pallas_call x1, Pallas kernels, local(): pl.pallas_call(kernel, out_shape=(pltpu.VMEM((1024, 512), jnp.float32), p...  55.4 us
    pallas_call x1, Pallas kernels, local(): pl.pallas_call(divide, out_shape=jax.ShapeDtypeStruct((1024, 512), jnp.fl...  1.34 us

profile of v5, /device:TPU:1, one launch (start us, length us, event | category | flops | bytes accessed | tf_op | source)
XLA Modules:
  0.0 56.8 jit_solution(5967299977708350993)
XLA Ops:
  0.0 55.4 %shard_map.37 = (f32[1024,512]{1,0:T(8,128)S(1)}, f32[1,512]{1,0:T(1,128)S(1)}) custom-call(s32[2,4]{1,0:T(2,128)} %bitcast.3, bf16[1024,512]{1,0:T(8,128)(2,1)} %weights_ref.1, bf16[4,256,512]{2,1,0:T(8,128)(2,1)} %bitcast.2), custom_call_target="tpu_custom_call" | custom-call | flops 8589934592 | bytes 4194304 | tf_op jit(solution)/shard_map/pallas_call | solution.py:342
  55.4 1.3 %shard_map.38 = f32[1024,512]{1,0:T(8,128)} custom-call(f32[1024,512]{1,0:T(8,128)S(1)} %get-tuple-element.7.inflated_ref, f32[1,512]{1,0:T(1,128)S(1)} %get-tuple-element.8.totals_ref), custom_call_target="tpu_custom_call" | custom-call | tf_op jit(solution)/shard_map/pallas_call | solution.py:382

commit v6 on v5

--- a/solution.py
+++ b/solution.py
@@ -8,7 +8,7 @@
 from jax.sharding import PartitionSpec as P
 
 TILE = 256
-HALF = 128
+CUTS = ((0, 192), (192, 64))
 MESH = pl.DeviceIdType.MESH
 SIDE = 4
 SLOTS = 4
@@ -84,7 +84,7 @@
 
 def kernel(
     pattern_ref, weights_ref, panel_ref, total, sums_ref,
-    own, left, graph, panel, pattern, meta, part, parts, local_sem,
+    own, left, graph, panel, pattern, meta, codes, part, parts, local_sem,
     a_send, a_recv, b_send, b_recv, c_send, c_recv, m_send, m_recv, t_send, t_recv, both,
 ):
     row, col = lax.axis_index("row"), lax.axis_index("col")
@@ -127,7 +127,9 @@
 
     load_p.wait()
     bits = [pattern[i % 2, i // 2] for i in range(8)]
-    meta[col, 0] = functools.reduce(lambda a, b: a + b, [bits[i] << i for i in range(8)])
+    number = functools.reduce(lambda a, b: a + b, [bits[i] << i for i in range(8)])
+    codes[col] = jnp.full((1, 128), number, jnp.int32)
+    meta[col] = number
     def places(have):
         gaps, extras = [jnp.int32(0)], [jnp.int32(0)]
         for i in range(3):
@@ -162,21 +164,19 @@
         for (dx, dz), (px, pz), first, count in PHASES[number]:
             tiles = graph.at[at(-px, -pz), pl.ds(first, count)]
             if number >= 7:
-                tiles = tiles.at[:, pl.ds((number - 7) * HALF, HALF)]
+                tiles = tiles.at[:, pl.ds(*CUTS[number - 7])]
             remote(tiles, tiles, a_send, a_recv.at[number], (row, at(dx - px, dz - pz))).start()
 
     def send_codes(number):
         for (dx, dz), (px, pz) in CODES[number]:
-            code = meta.at[at(-px, -pz)]
+            code = codes.at[at(-px, -pz)]
             remote(code, code, m_send, m_recv.at[number], (row, at(dx - px, dz - pz))).start()
 
     def a_wait(number):
         if number >= 7:
-            arrived(graph.at[0, pl.ds(0, 2)], a_recv.at[number])
+            arrived(graph.at[0, :, pl.ds(*CUTS[number - 7])], a_recv.at[number])
         else:
             arrived(graph.at[pl.ds(0, 2)], a_recv.at[number])
-        if number in CODES:
-            arrived(meta.at[pl.ds(0, len(CODES[number]))], m_recv.at[number])
 
     def two(device_row, j):
         return panel.at[pl.ds(device_row * 4 + j, 2)]
@@ -222,7 +222,7 @@
             for c in range(2))
 
     def code(source):
-        present = meta[source, 0]
+        present = meta[source]
         have = [(present >> i) & 1 for i in range(8)]
         return have, places(have)
 
@@ -236,22 +236,22 @@
             else:
                 total[rows, :] += value
 
-    def finish(source, half):
+    def finish(source, start, size):
         have, holding = code(source)
         for r in range(4):
             for c in range(2):
-                left[r * HALF:(r + 1) * HALF, c * TILE:(c + 1) * TILE] = unpacked(
-                    source, have, holding, 2 * r + c, half * HALF, HALF)
+                left[r * size:(r + 1) * size, c * TILE:(c + 1) * TILE] = unpacked(
+                    source, have, holding, 2 * r + c, start, size)
         piece = pl.multiple_of(source * 2, 2)
         right = panel[pl.ds(piece, 2)].reshape(2 * TILE, 512)
-        value = jnp.dot(left[...], right, preferred_element_type=jnp.float32)
+        value = jnp.dot(left[:4 * size], right, preferred_element_type=jnp.float32)
         sums = jnp.zeros((8, 512), jnp.float32)
         for r in range(4):
-            rows = pl.ds(r * TILE + half * HALF, HALF)
-            square = total[rows, :] + value[r * HALF:(r + 1) * HALF]
+            rows = pl.ds(r * TILE + start, size)
+            square = total[rows, :] + value[r * size:(r + 1) * size]
             square = square * square
             total[rows, :] = square
-            sums += jnp.sum(square.reshape(HALF // 8, 8, 512), axis=0)
+            sums += jnp.sum(square.reshape(size // 8, 8, 512), axis=0)
         return sums
 
     def own_pair(number, along):
@@ -272,10 +272,10 @@
     pack(2)
     pack(3)
     pl.semaphore_wait(both, 1)
+    send_codes(1)
     own_pair(0, 1 - core)
     own_pair(1, core)
     own_pair(1, 1 - core)
-    send_codes(1)
     load_b.wait()
     for step in (1, 2):
         for way in (1, -1):
@@ -287,10 +287,17 @@
     for (kind, number), count in zip(MOMENTS, COUNTS):
         if kind == "a":
             a_wait(number)
-            for later in {0: (2,), 1: (3,), 2: (4,), 3: (5, 6), 5: (7, 8)}.get(number, ()):
+            heard = {0: (1,), 2: (3, 6), 4: (5,), 6: (7,)}.get(number, ())
+            for phase in heard:
+                arrived(codes.at[pl.ds(0, len(CODES[phase]))], m_recv.at[phase])
+            for phase in {0: (3, 6), 2: (5,), 4: (7,)}.get(number, ()):
+                send_codes(phase)
+            for later in {0: (2,), 1: (3,), 2: (4,), 3: (5,), 4: (6,), 5: (7, 8)}.get(number, ()):
                 send(later)
-                if later in CODES:
-                    send_codes(later)
+            for phase in heard:
+                for (dx, dz), _ in CODES[phase]:
+                    source = at(-dx, -dz)
+                    meta[source] = jnp.max(codes[source])
         elif kind == "b":
             b_wait(number)
             for way in (1, -1):
@@ -305,7 +312,7 @@
                 add_source(ordered(done), done == 0)
             done += 1
         if kind == "a" and number >= 7:
-            sums.append(finish(ordered(SIDE * SIDE - 1), number - 7))
+            sums.append(finish(ordered(SIDE * SIDE - 1), *CUTS[number - 7]))
 
     sums = jnp.sum(sums[0] + sums[1], axis=0, keepdims=True)
     part[...] = sums
@@ -314,7 +321,7 @@
     parts[row] = sums
 
     sent(graph.at[pl.ds(0, 15)], a_send)
-    sent(meta.at[pl.ds(0, 15)], m_send)
+    sent(codes.at[pl.ds(0, 15)], m_send)
     sent(panel.at[pl.ds(0, 4 * STEPS)], b_send)
     sent(panel.at[pl.ds(0, 4 + 4 * STEPS)], c_send)
 
@@ -352,11 +359,12 @@
         ),
         scratch_shapes=[
             pltpu.VMEM((1024, 512), jnp.bfloat16),
-            pltpu.VMEM((4 * HALF, 2 * TILE), jnp.bfloat16),
+            pltpu.VMEM((4 * CUTS[0][1], 2 * TILE), jnp.bfloat16),
             pltpu.VMEM((16, SLOTS, TILE, TILE), jnp.bfloat16),
             pltpu.VMEM((32, TILE, 512), jnp.bfloat16),
             pltpu.SMEM((2, 4), jnp.int32),
-            pltpu.SMEM((16, 128), jnp.int32),
+            pltpu.SMEM((16,), jnp.int32),
+            pltpu.VMEM((16, 1, 128), jnp.int32),
             pltpu.VMEM((1, 512), jnp.float32),
             pltpu.VMEM((8, 1, 512), jnp.float32),
             pltpu.SemaphoreType.DMA((5,)),

time: 56.9 us -> 56.7 us (level)
  no operation moved by 1% of the time
where the time goes in v6:
time: 56.7 us; the launch traced here: 56.6 us
  Pallas kernels  56.6 us (100%)
    pallas_call x1, Pallas kernels, local(): pl.pallas_call(kernel, out_shape=(pltpu.VMEM((1024, 512), jnp.float32), p...  55.2 us
    pallas_call x1, Pallas kernels, local(): pl.pallas_call(divide, out_shape=jax.ShapeDtypeStruct((1024, 512), jnp.fl...  1.34 us

profile of v6, /device:TPU:1, one launch (start us, length us, event | category | flops | bytes accessed | tf_op | source)
XLA Modules:
  0.0 56.6 jit_solution(5624094122156076636)
XLA Ops:
  0.0 55.2 %shard_map.37 = (f32[1024,512]{1,0:T(8,128)S(1)}, f32[1,512]{1,0:T(1,128)S(1)}) custom-call(s32[2,4]{1,0:T(2,128)} %bitcast.3, bf16[1024,512]{1,0:T(8,128)(2,1)} %weights_ref.1, bf16[4,256,512]{2,1,0:T(8,128)(2,1)} %bitcast.2), custom_call_target="tpu_custom_call" | custom-call | flops 8589934592 | bytes 4194304 | tf_op jit(solution)/shard_map/pallas_call | solution.py:349
  55.2 1.3 %shard_map.38 = f32[1024,512]{1,0:T(8,128)} custom-call(f32[1024,512]{1,0:T(8,128)S(1)} %get-tuple-element.7.inflated_ref, f32[1,512]{1,0:T(1,128)S(1)} %get-tuple-element.8.totals_ref), custom_call_target="tpu_custom_call" | custom-call | tf_op jit(solution)/shard_map/pallas_call | solution.py:390

commit v7 on v6

--- a/solution.py
+++ b/solution.py
@@ -316,7 +316,7 @@
 
     sums = jnp.sum(sums[0] + sums[1], axis=0, keepdims=True)
     part[...] = sums
-    for i in range(1, 8):
+    for i in (4, 3, 5, 2, 6, 7, 1):
         remote(part, parts.at[row], t_send, t_recv, ((row + i) % 8, col)).start()
     parts[row] = sums
 

time: 56.7 us -> 56.6 us (level)
  no operation moved by 1% of the time
where the time goes in v7:
time: 56.6 us; the launch traced here: 56.5 us
  Pallas kernels  56.5 us (100%)
    pallas_call x1, Pallas kernels, local(): pl.pallas_call(kernel, out_shape=(pltpu.VMEM((1024, 512), jnp.float32), p...  55.1 us
    pallas_call x1, Pallas kernels, local(): pl.pallas_call(divide, out_shape=jax.ShapeDtypeStruct((1024, 512), jnp.fl...  1.34 us

profile of v7, /device:TPU:1, one launch (start us, length us, event | category | flops | bytes accessed | tf_op | source)
XLA Modules:
  0.0 56.5 jit_solution(17342859893779948756)
XLA Ops:
  0.0 55.1 %shard_map.37 = (f32[1024,512]{1,0:T(8,128)S(1)}, f32[1,512]{1,0:T(1,128)S(1)}) custom-call(s32[2,4]{1,0:T(2,128)} %bitcast.3, bf16[1024,512]{1,0:T(8,128)(2,1)} %weights_ref.1, bf16[4,256,512]{2,1,0:T(8,128)(2,1)} %bitcast.2), custom_call_target="tpu_custom_call" | custom-call | flops 8589934592 | bytes 4194304 | tf_op jit(solution)/shard_map/pallas_call | solution.py:349
  55.2 1.3 %shard_map.38 = f32[1024,512]{1,0:T(8,128)} custom-call(f32[1024,512]{1,0:T(8,128)S(1)} %get-tuple-element.7.inflated_ref, f32[1,512]{1,0:T(1,128)S(1)} %get-tuple-element.8.totals_ref), custom_call_target="tpu_custom_call" | custom-call | tf_op jit(solution)/shard_map/pallas_call | solution.py:390
